TPU v7x, 768 devices: a whole 4x8x12 slice. The times are simulated.
768 devices in a mesh: grid: 96 (over z_hi, x, y), depth: 8 (over z_lo, core).
Axes of the slice: x: 4, y: 8, z: 12 (z_hi: 3, z_lo: 4; z = z_hi * 4 + z_lo), core: 2. Of those that a mesh axis runs over, the one named last changes fastest.
Arguments:
- density: float32 [384, 8, 32, 32], P('grid', 'depth'), may hold values from -1 to 1
- columns: int32 [384, 8, 1], P('grid', 'depth'), may hold values from 0 to 47, as said below
- fill_columns: int32 [384, 8, 4], P('grid', 'depth'), may hold values from 0 to 47, as said below
Outputs:
- purified: float32 [384, 8, 32, 128], P('grid', 'depth')
Inputs may be any that keep to these rules, and one draw needn't show every extreme that they name: `columns`: the 1 entries of one block row and one column group are distinct. `fill_columns`: the 4 entries of one block row and one column group are distinct.
All inputs are finite; a program needn't handle non-finite values.
Results may differ from a plain program's by a relative error of at most 0.0003.
Values sent between devices are 32-bit elements; how exact they have to be, the bound alone decides.
No kernel may reach another device: no remote copies, remote signals or barrier semaphores. Data moves between devices by JAX's collectives and lax.ppermute only.
A program may use at most 32 MiB of HBM per device.

v0:
```python
import functools

import jax
import jax.numpy as jnp
from jax import lax
from jax.experimental import pallas as pl
from jax.experimental.pallas import tpu as pltpu
from jax.sharding import PartitionSpec as P

BS = 32
ROWS = 4
KF = 4
CB = 48
NCG = 8
LANES = 128
TILE = 40
NZ, NX, NYH, NYL, NL, NC = 3, 4, 4, 2, 4, 2
NY = NYH * NYL
FZ, FX, FY, FL = 2, 3, 2, 2


def turned(count, first):
    return [(n + first) % count for n in range(count)]


def device(zh, x, yh, yl):
    return ((zh * NX + x) * NYH + yh) * NYL + yl


FIRST = [
    [device(zh, x, yh, yl) for zh in turned(NZ, FZ) for yh in turned(NYH, FY)]
    for x in range(NX) for yl in range(NYL)
]
SECOND = [
    [device(zh, x, yh, yl) for x in turned(NX, FX) for yl in range(NYL)]
    for zh in range(NZ) for yh in range(NYH)
]
LINES = [[zl * NC + c for zl in turned(NL, FL)] for c in range(NC)]
PAIRS = [[zl * NC + c for c in range(NC)] for zl in range(NL)]
NP, NS = NZ * NYH, NX * NYL
PIECE = NP * BS + 16
GROUP = NCG * KF * BS


def place(slab, codes, wanted):
    lane_slot = lax.broadcasted_iota(jnp.int32, (8, LANES), 1) // BS
    blocks, columns = [], []
    for code in codes:
        keep = lane_slot == (code & 3)
        block = slab[pl.ds(pl.multiple_of(code >> 14, 8), BS), :].reshape(BS // 8, 8, LANES)
        column = jnp.broadcast_to(slab[pl.ds((code >> 2) & 4095, 1), :], (8, LANES))
        blocks.append(jnp.where(keep, block, 0.0))
        columns.append(jnp.where(keep, column, 0.0)[None])
    every = jnp.concatenate(blocks + columns).reshape(-1, LANES)
    every = every + pltpu.roll(every, 64, 1)
    every = every + pltpu.roll(every, 32, 1)
    count = len(codes)
    blocks = every[: count * BS].reshape(count, BS // 8, 8, LANES)
    columns = every[count * BS :].reshape(count, 8, LANES)
    lands = columns == jnp.stack(wanted)
    return jnp.where(lands[:, None], blocks, 0.0).reshape(count * BS, LANES)


def wanted_of(tile, row):
    return jnp.broadcast_to(tile[BS + 1 + row : BS + 2 + row, :], (8, LANES))


def halves(values, axis):
    high = values.astype(jnp.bfloat16)
    low = (values - high.astype(jnp.float32)).astype(jnp.bfloat16)
    return jnp.concatenate([high, low], axis=axis)


def product(total):
    return (total[:BS, :LANES] + total[:BS, LANES:]) + (total[BS:, :LANES] + total[BS:, LANES:])


def pack_kernel(columns, fill, density, out, copies):
    lane_slot = lax.broadcasted_iota(jnp.int32, (8, LANES), 1) // BS
    line = lax.broadcasted_iota(jnp.int32, (8, LANES), 0)
    numbers = jnp.zeros((8, LANES), jnp.int32)
    for slot in range(ROWS):
        numbers = jnp.where((line == 0) & (lane_slot == slot), columns[0, slot], numbers)
    for row in range(ROWS):
        for slot in range(KF):
            numbers = jnp.where((line == row + 1) & (lane_slot == slot), fill[row, slot], numbers)
    numbers = numbers.astype(jnp.float32)
    data = jnp.concatenate([density[row] for row in range(ROWS)], axis=1)
    out[:BS, :] = data
    out[BS:, :] = numbers
    for n in range(NP):
        copies[n, :BS, 0, :] = data
        copies[n, BS:, 0, :] = numbers[:1]


def spread_kernel(plane, out):
    for member in range(NP):
        block = plane[member, :BS, 0, :]
        column = plane[member, BS:, 0, :]
        for n in range(NS):
            out[n, member * BS : (member + 1) * BS, :] = block
            out[n, NP * BS + member : NP * BS + member + 1, :] = column
    for n in range(NS):
        out[n, NP * BS + NP :, :] = jnp.zeros((PIECE - NP * BS - NP, LANES), jnp.float32)


def square_kernel(codes, tile, left, slab, out, own, right):
    for row in range(0, ROWS, 2):
        wanted = [wanted_of(tile, row)] * NCG + [wanted_of(tile, row + 1)] * NCG
        blocks = place(slab, [codes[row * NCG + t] for t in range(2 * NCG)], wanted)
        right[row * NCG * BS : (row + 2) * NCG * BS, :] = halves(blocks, 1)
    for row in range(ROWS):
        values = right[row * NCG * BS : (row + 1) * NCG * BS, :]
        result = product(jnp.dot(halves(left[row], 0), values, preferred_element_type=jnp.float32))
        rows = slice(row * BS, (row + 1) * BS)
        own[rows, :] = result
        for n in range(NL):
            out[n, rows, :] = result


def right_kernel(start, codes, tile, slab, out):
    batch = 16
    for row in range(ROWS // 2):
        wanted = [wanted_of(tile, start + row)] * batch
        for t in range(row * NCG * KF, (row + 1) * NCG * KF, batch):
            blocks = place(slab, [codes[start * NCG * KF + t + n] for n in range(batch)], wanted)
            out[t * BS : (t + batch) * BS, :] = halves(blocks, 1)


def cube_kernel(mine, other, own, upper, lower, out):
    for row in range(ROWS):
        right = upper if row < ROWS // 2 else lower
        rows = slice(row * BS, (row + 1) * BS)
        total = jnp.zeros((2 * BS, 2 * LANES), jnp.float32)
        for near in range(NL):
            values = jnp.concatenate([mine[near, rows, :], other[near, rows, :]], axis=1)
            start = row % (ROWS // 2) * GROUP + near * NC * LANES
            total = total + jnp.dot(
                halves(values, 0), right[start : start + NC * LANES, :], preferred_element_type=jnp.float32
            )
        out[rows, :] = 3.0 * own[rows, :] - 2.0 * product(total)


def vmem():
    return pl.BlockSpec(memory_space=pltpu.VMEM)


def smem():
    return pl.BlockSpec(memory_space=pltpu.SMEM)


def call(kernel, name, shapes, specs, args, scratch=(), limit=16 * 2**20):
    size = 4 * sum(a.size for a in args)
    shapes = [jax.ShapeDtypeStruct(*shape) for shape in shapes]
    results = pl.pallas_call(
        kernel,
        out_shape=shapes,
        in_specs=specs,
        out_specs=[vmem() for _ in shapes],
        scratch_shapes=list(scratch),
        compiler_params=pltpu.CompilerParams(vmem_limit_bytes=limit),
        cost_estimate=pl.CostEstimate(flops=2**24, bytes_accessed=size, transcendentals=0),
        name=name,
    )(*args)
    return results if len(shapes) > 1 else results[0]


def codes_of(block_row):
    owner, slot = block_row // ROWS, block_row % ROWS
    piece = (owner // NY - FX) % NX * NYL + owner % NYL
    member = (owner // (NX * NY) - FZ) % NZ * NYH + (owner % NY // NYL - FY) % NYH
    return (piece * PIECE + member * BS) * 2**14 + (piece * PIECE + NP * BS + member) * 4 + slot


def local(density, columns, fill_columns):
    f32 = jnp.float32
    tile, copies = call(
        pack_kernel, "pack", [((TILE, LANES), f32), ((NP, BS + 1, 1, LANES), f32)], [smem(), smem(), vmem()],
        (columns.reshape(1, ROWS), fill_columns.reshape(ROWS, KF), density.reshape(ROWS, BS, BS)),
        limit=60 * 2**20,
    )
    plane = lax.all_to_all(copies, "grid", 0, 0, axis_index_groups=FIRST)
    pair = lax.all_gather(tile, "depth", axis_index_groups=PAIRS)
    plane, pair = lax.optimization_barrier((plane, pair))
    pieces = call(spread_kernel, "spread", [((NS, PIECE, LANES), f32)], [vmem()], (plane,))
    slab = lax.all_to_all(pieces, "grid", 0, 0, axis_index_groups=SECOND).reshape(NS * PIECE, LANES)

    near = [pair] + [
        lax.ppermute(pair, "depth", [(n, (n + step * NC) % NCG) for n in range(NCG)]) for step in range(1, NL)
    ]
    rows = jnp.stack(near).reshape(NCG, TILE, LANES)
    numbers = rows[:, BS : BS + 5, ::BS].astype(jnp.int32)
    place_here, core = lax.axis_index("depth") // NC, lax.axis_index("depth") % NC
    steps = jnp.arange(NCG, dtype=jnp.int32)
    groups = ((place_here - steps // NC) % NL * NC + steps % NC) * CB
    first = codes_of(numbers[:, 0, :].T + groups[None, :]).reshape(-1)
    second = codes_of(numbers[:, 1:, :].transpose(1, 0, 2) + groups[None, :, None])
    second = second.reshape(ROWS, NL, NC, KF)
    places, lines = jnp.arange(NL, dtype=jnp.int32), jnp.array(turned(NL, FL), dtype=jnp.int32)
    turn = ((place_here - lines[:, None]) % NL == places[None, :])[None, :, :, None, None]
    second = jnp.sum(jnp.where(turn, second[:, None], 0), axis=2)
    second = jnp.where(core == 0, second, second[:, :, ::-1]).reshape(-1)
    left = rows[:, :BS].reshape(NCG, BS, ROWS, BS).transpose(2, 1, 0, 3).reshape(ROWS, BS, NCG * BS)

    shape = (ROWS * BS, LANES)
    squared, own = call(
        square_kernel, "square", [((NL,) + shape, f32), (shape, f32)], [smem(), vmem(), vmem(), vmem()],
        (first, tile, left, slab),
        [pltpu.VMEM((ROWS * NCG * BS, 2 * LANES), jnp.bfloat16)],
    )
    upper, lower = (
        functools.partial(
            call, functools.partial(right_kernel, start), "right", [((ROWS // 2 * GROUP, 2 * LANES), jnp.bfloat16)],
            [smem(), vmem(), vmem()],
        )
        for start in (0, ROWS // 2)
    )
    mine, upper = lax.optimization_barrier((lax.all_to_all(squared, "depth", 0, 0, axis_index_groups=LINES), upper((second, tile, slab))))
    other = lax.ppermute(mine, "depth", [(n, n ^ 1) for n in range(NCG)])
    lower = lower((second, tile, slab))
    purified = call(cube_kernel, "cube", [(shape, f32)], [vmem()] * 5, (mine, other, own, upper, lower))
    return purified.reshape(ROWS, 1, BS, LANES)


def solution(mesh):
    blocks, pattern = P("grid", "depth", None, None), P("grid", "depth", None)
    return jax.shard_map(
        local, mesh=mesh, in_specs=(blocks, pattern, pattern), out_specs=blocks, check_vma=False
    )
```

profile of v0, /device:TPU:1, one launch (start us, length us, event | category | flops | bytes accessed | tf_op | source)
XLA Modules:
  0.0 75.5 jit_solution(17744175505434604974)
XLA Ops:
  0.0 1.7 %pack.1 = (f32[40,128]{1,0:T(8,128)}, f32[12,33,1,128]{3,2,1,0:T(1,128)}) custom-call(s32[1,4]{1,0:T(1,128)} %bitcast.69, s32[4,4]{1,0:T(4,128)} %bitcast.68, f32[4,32,32]{2,1,0:T(8,128)} %bitcast.63), custom_call_target="tpu_custom_call" | custom-call | flops 16777216 | bytes 16464 | tf_op jit(solution)/shard_map/pack/pallas_call | solution.py:155
  1.7 21.9 %all-to-all-start = ((f32[12,33,1,128]{3,2,1,0:T(1,128)}), f32[12,33,1,128]{3,2,1,0:T(1,128)S(1)}, u32[]{:S(2)}, u32[]{:S(2)}) async-start(f32[12,33,1,128]{3,2,1,0:T(1,128)} %get-tuple-element.13), calls=%async_computation | async-start | bytes 405504 | tf_op jit(solution)/shard_map/all_to_all | solution.py:182
  23.6 2.6 %all-gather = f32[80,128]{1,0:T(8,128)S(1)} all-gather(f32[40,128]{1,0:T(8,128)} %get-tuple-element.14.tile), channel_id=2, replica_groups={{0,1},{2,3},{4,5},{6,7},{8,9},{10,11},{12,13},{14,15},{16,17},{18,19},{..., dimensions={0}, use_global_device_ids=true | all-gather | bytes 61440 | tf_op jit(solution)/shard_map/all_gather | solution.py:183
  26.2 2.1 %all-to-all-done.plane = f32[12,33,1,128]{3,2,1,0:T(1,128)S(1)} async-done(((f32[12,33,1,128]{3,2,1,0:T(1,128)}), f32[12,33,1,128]{3,2,1,0:T(1,128)S(1)}, u32[]{:S(2)}, u32[]{:S(2)}) %all-to-all-start) | async-done | bytes 202784 | tf_op jit(solution)/shard_map/all_to_all | solution.py:182
  28.4 1.3 %spread.1 = f32[8,400,128]{2,1,0:T(8,128)} custom-call(f32[12,33,1,128]{3,2,1,0:T(1,128)S(1)} %all-to-all-done.plane), custom_call_target="tpu_custom_call" | custom-call | flops 16777216 | bytes 202752 | tf_op jit(solution)/shard_map/spread/pallas_call | solution.py:155
  29.7 0.0 copy-start.1
  29.7 6.1 %all-to-all-start.1 = ((f32[8,400,128]{2,1,0:T(8,128)}), f32[8,400,128]{2,1,0:T(8,128)S(1)}, u32[]{:S(2)}, u32[]{:S(2)}) async-start(f32[8,400,128]{2,1,0:T(8,128)} %spread.1), calls=%async_computation.1 | async-start | bytes 3276800 | tf_op jit(solution)/shard_map/all_to_all | solution.py:186
  35.8 0.0 copy-done.1
  35.8 7.7 %collective-permute-start.2 = (f32[2,40,128]{2,1,0:T(8,128)S(1)}, f32[2,40,128]{2,1,0:T(8,128)S(1)}, u32[]{:S(2)}, u32[]{:S(2)}) collective-permute-start(f32[2,40,128]{2,1,0:T(8,128)S(1)} %bitcast.56), channel_id=1, source_target_pairs={{0,6},{1,7},{2,0},{3,1},{4,2},{5,3},{6,4},{7,5},{8,14},{9,15},{10,... | collective-permute-start | bytes 122888 | tf_op jit(solution)/shard_map/ppermute | solution.py:189
  43.5 1.9 %collective-permute-start.1 = (f32[2,40,128]{2,1,0:T(8,128)S(1)}, f32[2,40,128]{2,1,0:T(8,128)S(1)}, u32[]{:S(2)}, u32[]{:S(2)}) collective-permute-start(f32[2,40,128]{2,1,0:T(8,128)S(1)} %bitcast.57), channel_id=1, source_target_pairs={{0,4},{1,5},{2,6},{3,7},{4,0},{5,1},{6,2},{7,3},{8,12},{9,13},{10,... | collective-permute-start | bytes 122888 | tf_op jit(solution)/shard_map/ppermute | solution.py:189
  45.5 2.2 %collective-permute-start = (f32[2,40,128]{2,1,0:T(8,128)S(1)}, f32[2,40,128]{2,1,0:T(8,128)S(1)}, u32[]{:S(2)}, u32[]{:S(2)}) collective-permute-start(f32[2,40,128]{2,1,0:T(8,128)S(1)} %bitcast.58), channel_id=1, source_target_pairs={{0,2},{1,3},{2,4},{3,5},{4,6},{5,7},{6,0},{7,1},{8,10},{9,11},{10,... | collective-permute-start | bytes 122888 | tf_op jit(solution)/shard_map/ppermute | solution.py:189
  47.7 0.0 collective-permute-done.2
  47.7 1.8 %collective-permute-done.1 = f32[2,40,128]{2,1,0:T(8,128)S(1)} collective-permute-done((f32[2,40,128]{2,1,0:T(8,128)S(1)}, f32[2,40,128]{2,1,0:T(8,128)S(1)}, u32[]{:S(2)}, u32[]{:S(2)}) %collective-permute-start.1) | collective-permute-done | bytes 40992 | tf_op jit(solution)/shard_map/ppermute | solution.py:189
  49.5 2.8 %collective-permute-done = f32[2,40,128]{2,1,0:T(8,128)S(1)} collective-permute-done((f32[2,40,128]{2,1,0:T(8,128)S(1)}, f32[2,40,128]{2,1,0:T(8,128)S(1)}, u32[]{:S(2)}, u32[]{:S(2)}) %collective-permute-start) | collective-permute-done | bytes 40992 | tf_op jit(solution)/shard_map/ppermute | solution.py:189
  52.3 0.0 copy-start
  52.3 0.1 copy.9
  52.4 0.1 slice.12
  52.5 0.1 copy.10
  52.7 0.1 reshape.133.codes
  52.7 0.3 reshape.134
  53.1 0.2 reshape.135.left
  53.2 0.0 all-to-all-done.1
  53.3 0.0 copy-done
  53.3 1.9 %square.1 = (f32[4,128,128]{2,1,0:T(8,128)}, f32[128,128]{1,0:T(8,128)S(1)}) custom-call(s32[32]{0:T(128)S(1)} %reshape.133.codes, f32[40,128]{1,0:T(8,128)S(1)} %copy-done, f32[4,32,256]{2,1,0:T(8,128)S(1)} %reshape.135.left, f32[3200,128]{1,0:T(8,128)S(1)} %bitcast.50), custom_call_target="tpu_custom_call" | custom-call | flops 16777216 | bytes 1790080 | tf_op jit(solution)/shard_map/square/pallas_call | solution.py:155
  55.1 8.8 %all-to-all-start.2 = ((f32[4,128,128]{2,1,0:T(8,128)}), f32[4,128,128]{2,1,0:T(8,128)S(1)}, u32[]{:S(2)}, u32[]{:S(2)}) async-start(f32[4,128,128]{2,1,0:T(8,128)} %get-tuple-element.17), calls=%async_computation.2 | async-start | bytes 524288 | tf_op jit(solution)/shard_map/all_to_all | solution.py:218
  63.9 0.1 iota_compare_fusion
  63.9 0.2 fusion.13
  64.1 0.1 select_reduce_fusion
  64.3 0.1 reshape.137.codes
  64.4 1.4 %right.2.upper = bf16[2048,256]{1,0:T(8,128)(2,1)S(1)} custom-call(s32[128]{0:T(128)S(1)} %reshape.137.codes, f32[40,128]{1,0:T(8,128)S(1)} %copy-done, f32[3200,128]{1,0:T(8,128)S(1)} %bitcast.51), custom_call_target="tpu_custom_call" | custom-call | flops 16777216 | bytes 1659392 | tf_op jit(solution)/shard_map/right/pallas_call | solution.py:155
  65.8 1.8 %all-to-all-done.2.mine = f32[4,128,128]{2,1,0:T(8,128)S(1)} async-done(((f32[4,128,128]{2,1,0:T(8,128)}), f32[4,128,128]{2,1,0:T(8,128)S(1)}, u32[]{:S(2)}, u32[]{:S(2)}) %all-to-all-start.2) | async-done | bytes 262176 | tf_op jit(solution)/shard_map/all_to_all | solution.py:218
  67.6 5.4 %collective-permute-start.3 = (f32[4,128,128]{2,1,0:T(8,128)S(1)}, f32[4,128,128]{2,1,0:T(8,128)S(1)}, u32[]{:S(2)}, u32[]{:S(2)}) collective-permute-start(f32[4,128,128]{2,1,0:T(8,128)S(1)} %all-to-all-done.2.mine), channel_id=1, source_target_pairs={{0,1},{1,0},{2,3},{3,2},{4,5},{5,4},{6,7},{7,6},{8,9},{9,8},{10,11... | collective-permute-start | bytes 786440 | tf_op jit(solution)/shard_map/ppermute | solution.py:219
  73.0 1.4 %right.3.lower = bf16[2048,256]{1,0:T(8,128)(2,1)S(1)} custom-call(s32[128]{0:T(128)S(1)} %reshape.137.codes, f32[40,128]{1,0:T(8,128)S(1)} %copy-done, f32[3200,128]{1,0:T(8,128)S(1)} %bitcast.52), custom_call_target="tpu_custom_call" | custom-call | flops 16777216 | bytes 1659392 | tf_op jit(solution)/shard_map/right/pallas_call | solution.py:155
  74.3 0.0 collective-permute-done.3.other
  74.3 1.1 %cube.1 = f32[128,128]{1,0:T(8,128)} custom-call(f32[4,128,128]{2,1,0:T(8,128)S(1)} %all-to-all-done.2.mine, f32[4,128,128]{2,1,0:T(8,128)S(1)} %collective-permute-done.3.other, f32[128,128]{1,0:T(8,128)S(1)} %get-tuple-element.19.own, bf16[2048,256]{1,0:T(8,128)(2,1)S(1)} %right.2.upper, bf16[2048,256]{1,0:T(8,128)(2,1)S(1)} %right.3.lower), custom_call_target="tpu_custom_call" | custom-call | flops 16777216 | bytes 4784128 | tf_op jit(solution)/shard_map/cube/pallas_call | solution.py:155
  (11 shorter events, 0.2 us)
Async XLA Ops:
  1.7 26.6 %all-to-all-start = ((f32[12,33,1,128]{3,2,1,0:T(1,128)}), f32[12,33,1,128]{3,2,1,0:T(1,128)S(1)}, u32[]{:S(2)}, u32[]{:S(2)}) async-start(f32[12,33,1,128]{3,2,1,0:T(1,128)} %get-tuple-element.13), calls=%async_computation | async-start | bytes 405504 | tf_op jit(solution)/shard_map/all_to_all | solution.py:182
  29.7 6.1 %copy-start.1 = (s32[4]{0:T(128)S(1)}, s32[4]{0:T(128)}, u32[]{:S(2)}) copy-start(s32[4]{0:T(128)} %constant.248) | copy-start | bytes 52
  29.7 23.6 %all-to-all-start.1 = ((f32[8,400,128]{2,1,0:T(8,128)}), f32[8,400,128]{2,1,0:T(8,128)S(1)}, u32[]{:S(2)}, u32[]{:S(2)}) async-start(f32[8,400,128]{2,1,0:T(8,128)} %spread.1), calls=%async_computation.1 | async-start | bytes 3276800 | tf_op jit(solution)/shard_map/all_to_all | solution.py:186
  35.8 11.9 %collective-permute-start.2 = (f32[2,40,128]{2,1,0:T(8,128)S(1)}, f32[2,40,128]{2,1,0:T(8,128)S(1)}, u32[]{:S(2)}, u32[]{:S(2)}) collective-permute-start(f32[2,40,128]{2,1,0:T(8,128)S(1)} %bitcast.56), channel_id=1, source_target_pairs={{0,6},{1,7},{2,0},{3,1},{4,2},{5,3},{6,4},{7,5},{8,14},{9,15},{10,... | collective-permute-start | bytes 122888 | tf_op jit(solution)/shard_map/ppermute | solution.py:189
  43.5 5.9 %collective-permute-start.1 = (f32[2,40,128]{2,1,0:T(8,128)S(1)}, f32[2,40,128]{2,1,0:T(8,128)S(1)}, u32[]{:S(2)}, u32[]{:S(2)}) collective-permute-start(f32[2,40,128]{2,1,0:T(8,128)S(1)} %bitcast.57), channel_id=1, source_target_pairs={{0,4},{1,5},{2,6},{3,7},{4,0},{5,1},{6,2},{7,3},{8,12},{9,13},{10,... | collective-permute-start | bytes 122888 | tf_op jit(solution)/shard_map/ppermute | solution.py:189
  45.5 6.8 %collective-permute-start = (f32[2,40,128]{2,1,0:T(8,128)S(1)}, f32[2,40,128]{2,1,0:T(8,128)S(1)}, u32[]{:S(2)}, u32[]{:S(2)}) collective-permute-start(f32[2,40,128]{2,1,0:T(8,128)S(1)} %bitcast.58), channel_id=1, source_target_pairs={{0,2},{1,3},{2,4},{3,5},{4,6},{5,7},{6,0},{7,1},{8,10},{9,11},{10,... | collective-permute-start | bytes 122888 | tf_op jit(solution)/shard_map/ppermute | solution.py:189
  52.3 1.0 %copy-start = (f32[40,128]{1,0:T(8,128)S(1)}, f32[40,128]{1,0:T(8,128)}, u32[]{:S(2)}) copy-start(f32[40,128]{1,0:T(8,128)} %get-tuple-element.14.tile) | copy-start | bytes 61444
  55.1 12.5 %all-to-all-start.2 = ((f32[4,128,128]{2,1,0:T(8,128)}), f32[4,128,128]{2,1,0:T(8,128)S(1)}, u32[]{:S(2)}, u32[]{:S(2)}) async-start(f32[4,128,128]{2,1,0:T(8,128)} %get-tuple-element.17), calls=%async_computation.2 | async-start | bytes 524288 | tf_op jit(solution)/shard_map/all_to_all | solution.py:218
  67.6 6.7 %collective-permute-start.3 = (f32[4,128,128]{2,1,0:T(8,128)S(1)}, f32[4,128,128]{2,1,0:T(8,128)S(1)}, u32[]{:S(2)}, u32[]{:S(2)}) collective-permute-start(f32[4,128,128]{2,1,0:T(8,128)S(1)} %all-to-all-done.2.mine), channel_id=1, source_target_pairs={{0,1},{1,0},{2,3},{3,2},{4,5},{5,4},{6,7},{7,6},{8,9},{9,8},{10,11... | collective-permute-start | bytes 786440 | tf_op jit(solution)/shard_map/ppermute | solution.py:219
where the time goes:
time: 76 us; the launch traced here: 75.5 us
  starting transfers between devices  53.9 us (71%)
  Pallas kernels  8.75 us (12%)
  waiting for transfers between devices  8.55 us (11%)
  blocking collectives  2.65 us (3%)
  local copies, waits for them, and re-layouts  1 us (1%)
    all_to_all x1, starting transfers between devices, local(): plane = lax.all_to_all(copies, 'grid', 0, 0, axis_index_groups=FIRST)  21.9 us
    ppermute x3, starting transfers between devices, local(): lax.ppermute(pair, 'depth', [(n, (n + step * NC) % NCG) for n in range(NC...  11.8 us
    all_to_all x1, starting transfers between devices, local(): lax.all_to_all(squared, 'depth', 0, 0, axis_index_groups=LINES)  8.76 us
    pallas_call x6, Pallas kernels, call(): pl.pallas_call(kernel, out_shape=shapes, in_specs=specs, out_specs=[vmem(...  8.75 us
    all_to_all x1, starting transfers between devices, local(): lax.all_to_all(pieces, 'grid', 0, 0, axis_index_groups=SECOND)  6.1 us
    ppermute x1, starting transfers between devices, local(): other = lax.ppermute(mine, 'depth', [(n, n ^ 1) for n in range(NCG)])  5.36 us
    ppermute x3, waiting for transfers between devices, local(): lax.ppermute(pair, 'depth', [(n, (n + step * NC) % NCG) for n in range(NC...  4.61 us
    all_gather x1, blocking collectives, local(): pair = lax.all_gather(tile, 'depth', axis_index_groups=PAIRS)  2.65 us
  transfers between devices with their start and end apart: 7, of which 4 were waited for; matrix products, arithmetic and copies ran while one was open for 2% of the time, Pallas kernels for 4%

commit v1 on v0

--- a/solution.py
+++ b/solution.py
@@ -16,7 +16,7 @@
 TILE = 40
 NZ, NX, NYH, NYL, NL, NC = 3, 4, 4, 2, 4, 2
 NY = NYH * NYL
-FZ, FX, FY, FL = 2, 3, 2, 2
+FZ, FX, FY, FL = 2, 3, 3, 2
 
 
 def turned(count, first):

time: 76 us -> 75.3 us (level)
  starting transfers between devices: 53.9 us -> 51.2 us
  waiting for transfers between devices: 8.55 us -> 10.5 us
    all_to_all x1, waiting for transfers between devices: 2.13 us -> 4.16 us  [local(): plane = lax.all_to_all(copies, 'grid', 0, 0, axis_index_groups=FIRST)]
    all_to_all x1, starting transfers between devices: 21.9 us -> 20.3 us  [local(): plane = lax.all_to_all(copies, 'grid', 0, 0, axis_index_groups=FIRST)]
    ppermute x3, starting transfers between devices: 11.8 us -> 11 us  [local(): lax.ppermute(pair, 'depth', [(n, (n + step * NC) % NCG) for n in range(NC...]
where the time goes in v1:
time: 75.3 us; the launch traced here: 74.8 us
  starting transfers between devices  51.2 us (68%)
  waiting for transfers between devices  10.5 us (14%)
  Pallas kernels  8.75 us (12%)
  blocking collectives  2.66 us (4%)
  local copies, waits for them, and re-layouts  1 us (1%)
    all_to_all x1, starting transfers between devices, local(): plane = lax.all_to_all(copies, 'grid', 0, 0, axis_index_groups=FIRST)  20.3 us
    ppermute x3, starting transfers between devices, local(): lax.ppermute(pair, 'depth', [(n, (n + step * NC) % NCG) for n in range(NC...  11 us
    pallas_call x6, Pallas kernels, call(): pl.pallas_call(kernel, out_shape=shapes, in_specs=specs, out_specs=[vmem(...  8.75 us
    all_to_all x1, starting transfers between devices, local(): lax.all_to_all(squared, 'depth', 0, 0, axis_index_groups=LINES)  8.05 us
    all_to_all x1, starting transfers between devices, local(): lax.all_to_all(pieces, 'grid', 0, 0, axis_index_groups=SECOND)  6.1 us
    ppermute x1, starting transfers between devices, local(): other = lax.ppermute(mine, 'depth', [(n, n ^ 1) for n in range(NCG)])  5.79 us
    ppermute x3, waiting for transfers between devices, local(): lax.ppermute(pair, 'depth', [(n, (n + step * NC) % NCG) for n in range(NC...  4.61 us
    all_to_all x1, waiting for transfers between devices, local(): plane = lax.all_to_all(copies, 'grid', 0, 0, axis_index_groups=FIRST)  4.16 us
  transfers between devices with their start and end apart: 7, of which 4 were waited for; matrix products, arithmetic and copies ran while one was open for 2% of the time, Pallas kernels for 4%

profile of v1, /device:TPU:1, one launch (start us, length us, event | category | flops | bytes accessed | tf_op | source)
XLA Modules:
  0.0 74.8 jit_solution(3122518688816353411)
XLA Ops:
  0.0 1.7 %pack.1 = (f32[40,128]{1,0:T(8,128)}, f32[12,33,1,128]{3,2,1,0:T(1,128)}) custom-call(s32[1,4]{1,0:T(1,128)} %bitcast.69, s32[4,4]{1,0:T(4,128)} %bitcast.68, f32[4,32,32]{2,1,0:T(8,128)} %bitcast.63), custom_call_target="tpu_custom_call" | custom-call | flops 16777216 | bytes 16464 | tf_op jit(solution)/shard_map/pack/pallas_call | solution.py:155
  1.7 20.3 %all-to-all-start = ((f32[12,33,1,128]{3,2,1,0:T(1,128)}), f32[12,33,1,128]{3,2,1,0:T(1,128)S(1)}, u32[]{:S(2)}, u32[]{:S(2)}) async-start(f32[12,33,1,128]{3,2,1,0:T(1,128)} %get-tuple-element.13), calls=%async_computation | async-start | bytes 405504 | tf_op jit(solution)/shard_map/all_to_all | solution.py:182
  22.0 2.7 %all-gather = f32[80,128]{1,0:T(8,128)S(1)} all-gather(f32[40,128]{1,0:T(8,128)} %get-tuple-element.14.tile), channel_id=2, replica_groups={{0,1},{2,3},{4,5},{6,7},{8,9},{10,11},{12,13},{14,15},{16,17},{18,19},{..., dimensions={0}, use_global_device_ids=true | all-gather | bytes 61440 | tf_op jit(solution)/shard_map/all_gather | solution.py:183
  24.7 4.2 %all-to-all-done.plane = f32[12,33,1,128]{3,2,1,0:T(1,128)S(1)} async-done(((f32[12,33,1,128]{3,2,1,0:T(1,128)}), f32[12,33,1,128]{3,2,1,0:T(1,128)S(1)}, u32[]{:S(2)}, u32[]{:S(2)}) %all-to-all-start) | async-done | bytes 202784 | tf_op jit(solution)/shard_map/all_to_all | solution.py:182
  28.8 1.3 %spread.1 = f32[8,400,128]{2,1,0:T(8,128)} custom-call(f32[12,33,1,128]{3,2,1,0:T(1,128)S(1)} %all-to-all-done.plane), custom_call_target="tpu_custom_call" | custom-call | flops 16777216 | bytes 202752 | tf_op jit(solution)/shard_map/spread/pallas_call | solution.py:155
  30.1 0.0 copy-start.1
  30.1 6.1 %all-to-all-start.1 = ((f32[8,400,128]{2,1,0:T(8,128)}), f32[8,400,128]{2,1,0:T(8,128)S(1)}, u32[]{:S(2)}, u32[]{:S(2)}) async-start(f32[8,400,128]{2,1,0:T(8,128)} %spread.1), calls=%async_computation.1 | async-start | bytes 3276800 | tf_op jit(solution)/shard_map/all_to_all | solution.py:186
  36.3 0.0 copy-done.1
  36.3 6.9 %collective-permute-start.2 = (f32[2,40,128]{2,1,0:T(8,128)S(1)}, f32[2,40,128]{2,1,0:T(8,128)S(1)}, u32[]{:S(2)}, u32[]{:S(2)}) collective-permute-start(f32[2,40,128]{2,1,0:T(8,128)S(1)} %bitcast.56), channel_id=1, source_target_pairs={{0,6},{1,7},{2,0},{3,1},{4,2},{5,3},{6,4},{7,5},{8,14},{9,15},{10,... | collective-permute-start | bytes 122888 | tf_op jit(solution)/shard_map/ppermute | solution.py:189
  43.2 1.9 %collective-permute-start.1 = (f32[2,40,128]{2,1,0:T(8,128)S(1)}, f32[2,40,128]{2,1,0:T(8,128)S(1)}, u32[]{:S(2)}, u32[]{:S(2)}) collective-permute-start(f32[2,40,128]{2,1,0:T(8,128)S(1)} %bitcast.57), channel_id=1, source_target_pairs={{0,4},{1,5},{2,6},{3,7},{4,0},{5,1},{6,2},{7,3},{8,12},{9,13},{10,... | collective-permute-start | bytes 122888 | tf_op jit(solution)/shard_map/ppermute | solution.py:189
  45.1 2.2 %collective-permute-start = (f32[2,40,128]{2,1,0:T(8,128)S(1)}, f32[2,40,128]{2,1,0:T(8,128)S(1)}, u32[]{:S(2)}, u32[]{:S(2)}) collective-permute-start(f32[2,40,128]{2,1,0:T(8,128)S(1)} %bitcast.58), channel_id=1, source_target_pairs={{0,2},{1,3},{2,4},{3,5},{4,6},{5,7},{6,0},{7,1},{8,10},{9,11},{10,... | collective-permute-start | bytes 122888 | tf_op jit(solution)/shard_map/ppermute | solution.py:189
  47.3 0.0 collective-permute-done.2
  47.3 1.8 %collective-permute-done.1 = f32[2,40,128]{2,1,0:T(8,128)S(1)} collective-permute-done((f32[2,40,128]{2,1,0:T(8,128)S(1)}, f32[2,40,128]{2,1,0:T(8,128)S(1)}, u32[]{:S(2)}, u32[]{:S(2)}) %collective-permute-start.1) | collective-permute-done | bytes 40992 | tf_op jit(solution)/shard_map/ppermute | solution.py:189
  49.1 2.8 %collective-permute-done = f32[2,40,128]{2,1,0:T(8,128)S(1)} collective-permute-done((f32[2,40,128]{2,1,0:T(8,128)S(1)}, f32[2,40,128]{2,1,0:T(8,128)S(1)}, u32[]{:S(2)}, u32[]{:S(2)}) %collective-permute-start) | collective-permute-done | bytes 40992 | tf_op jit(solution)/shard_map/ppermute | solution.py:189
  51.9 0.0 copy-start
  52.0 0.1 copy.9
  52.0 0.1 slice.12
  52.2 0.1 copy.10
  52.3 0.1 reshape.133.codes
  52.4 0.3 reshape.134
  52.7 0.2 reshape.135.left
  52.9 0.0 all-to-all-done.1
  52.9 0.0 copy-done
  52.9 1.9 %square.1 = (f32[4,128,128]{2,1,0:T(8,128)}, f32[128,128]{1,0:T(8,128)S(1)}) custom-call(s32[32]{0:T(128)S(1)} %reshape.133.codes, f32[40,128]{1,0:T(8,128)S(1)} %copy-done, f32[4,32,256]{2,1,0:T(8,128)S(1)} %reshape.135.left, f32[3200,128]{1,0:T(8,128)S(1)} %bitcast.50), custom_call_target="tpu_custom_call" | custom-call | flops 16777216 | bytes 1790080 | tf_op jit(solution)/shard_map/square/pallas_call | solution.py:155
  54.8 8.1 %all-to-all-start.2 = ((f32[4,128,128]{2,1,0:T(8,128)}), f32[4,128,128]{2,1,0:T(8,128)S(1)}, u32[]{:S(2)}, u32[]{:S(2)}) async-start(f32[4,128,128]{2,1,0:T(8,128)} %get-tuple-element.17), calls=%async_computation.2 | async-start | bytes 524288 | tf_op jit(solution)/shard_map/all_to_all | solution.py:218
  62.8 0.1 iota_compare_fusion
  62.9 0.2 fusion.13
  63.1 0.1 select_reduce_fusion
  63.2 0.1 reshape.137.codes
  63.4 1.4 %right.2.upper = bf16[2048,256]{1,0:T(8,128)(2,1)S(1)} custom-call(s32[128]{0:T(128)S(1)} %reshape.137.codes, f32[40,128]{1,0:T(8,128)S(1)} %copy-done, f32[3200,128]{1,0:T(8,128)S(1)} %bitcast.51), custom_call_target="tpu_custom_call" | custom-call | flops 16777216 | bytes 1659392 | tf_op jit(solution)/shard_map/right/pallas_call | solution.py:155
  64.7 1.8 %all-to-all-done.2.mine = f32[4,128,128]{2,1,0:T(8,128)S(1)} async-done(((f32[4,128,128]{2,1,0:T(8,128)}), f32[4,128,128]{2,1,0:T(8,128)S(1)}, u32[]{:S(2)}, u32[]{:S(2)}) %all-to-all-start.2) | async-done | bytes 262176 | tf_op jit(solution)/shard_map/all_to_all | solution.py:218
  66.5 5.8 %collective-permute-start.3 = (f32[4,128,128]{2,1,0:T(8,128)S(1)}, f32[4,128,128]{2,1,0:T(8,128)S(1)}, u32[]{:S(2)}, u32[]{:S(2)}) collective-permute-start(f32[4,128,128]{2,1,0:T(8,128)S(1)} %all-to-all-done.2.mine), channel_id=1, source_target_pairs={{0,1},{1,0},{2,3},{3,2},{4,5},{5,4},{6,7},{7,6},{8,9},{9,8},{10,11... | collective-permute-start | bytes 786440 | tf_op jit(solution)/shard_map/ppermute | solution.py:219
  72.3 1.4 %right.3.lower = bf16[2048,256]{1,0:T(8,128)(2,1)S(1)} custom-call(s32[128]{0:T(128)S(1)} %reshape.137.codes, f32[40,128]{1,0:T(8,128)S(1)} %copy-done, f32[3200,128]{1,0:T(8,128)S(1)} %bitcast.52), custom_call_target="tpu_custom_call" | custom-call | flops 16777216 | bytes 1659392 | tf_op jit(solution)/shard_map/right/pallas_call | solution.py:155
  73.7 0.0 collective-permute-done.3.other
  73.7 1.1 %cube.1 = f32[128,128]{1,0:T(8,128)} custom-call(f32[4,128,128]{2,1,0:T(8,128)S(1)} %all-to-all-done.2.mine, f32[4,128,128]{2,1,0:T(8,128)S(1)} %collective-permute-done.3.other, f32[128,128]{1,0:T(8,128)S(1)} %get-tuple-element.19.own, bf16[2048,256]{1,0:T(8,128)(2,1)S(1)} %right.2.upper, bf16[2048,256]{1,0:T(8,128)(2,1)S(1)} %right.3.lower), custom_call_target="tpu_custom_call" | custom-call | flops 16777216 | bytes 4784128 | tf_op jit(solution)/shard_map/cube/pallas_call | solution.py:155
  (11 shorter events, 0.2 us)
Async XLA Ops:
  1.7 27.1 %all-to-all-start = ((f32[12,33,1,128]{3,2,1,0:T(1,128)}), f32[12,33,1,128]{3,2,1,0:T(1,128)S(1)}, u32[]{:S(2)}, u32[]{:S(2)}) async-start(f32[12,33,1,128]{3,2,1,0:T(1,128)} %get-tuple-element.13), calls=%async_computation | async-start | bytes 405504 | tf_op jit(solution)/shard_map/all_to_all | solution.py:182
  30.1 6.1 %copy-start.1 = (s32[4]{0:T(128)S(1)}, s32[4]{0:T(128)}, u32[]{:S(2)}) copy-start(s32[4]{0:T(128)} %constant.248) | copy-start | bytes 52
  30.1 22.7 %all-to-all-start.1 = ((f32[8,400,128]{2,1,0:T(8,128)}), f32[8,400,128]{2,1,0:T(8,128)S(1)}, u32[]{:S(2)}, u32[]{:S(2)}) async-start(f32[8,400,128]{2,1,0:T(8,128)} %spread.1), calls=%async_computation.1 | async-start | bytes 3276800 | tf_op jit(solution)/shard_map/all_to_all | solution.py:186
  36.3 11.1 %collective-permute-start.2 = (f32[2,40,128]{2,1,0:T(8,128)S(1)}, f32[2,40,128]{2,1,0:T(8,128)S(1)}, u32[]{:S(2)}, u32[]{:S(2)}) collective-permute-start(f32[2,40,128]{2,1,0:T(8,128)S(1)} %bitcast.56), channel_id=1, source_target_pairs={{0,6},{1,7},{2,0},{3,1},{4,2},{5,3},{6,4},{7,5},{8,14},{9,15},{10,... | collective-permute-start | bytes 122888 | tf_op jit(solution)/shard_map/ppermute | solution.py:189
  43.2 5.9 %collective-permute-start.1 = (f32[2,40,128]{2,1,0:T(8,128)S(1)}, f32[2,40,128]{2,1,0:T(8,128)S(1)}, u32[]{:S(2)}, u32[]{:S(2)}) collective-permute-start(f32[2,40,128]{2,1,0:T(8,128)S(1)} %bitcast.57), channel_id=1, source_target_pairs={{0,4},{1,5},{2,6},{3,7},{4,0},{5,1},{6,2},{7,3},{8,12},{9,13},{10,... | collective-permute-start | bytes 122888 | tf_op jit(solution)/shard_map/ppermute | solution.py:189
  45.1 6.8 %collective-permute-start = (f32[2,40,128]{2,1,0:T(8,128)S(1)}, f32[2,40,128]{2,1,0:T(8,128)S(1)}, u32[]{:S(2)}, u32[]{:S(2)}) collective-permute-start(f32[2,40,128]{2,1,0:T(8,128)S(1)} %bitcast.58), channel_id=1, source_target_pairs={{0,2},{1,3},{2,4},{3,5},{4,6},{5,7},{6,0},{7,1},{8,10},{9,11},{10,... | collective-permute-start | bytes 122888 | tf_op jit(solution)/shard_map/ppermute | solution.py:189
  51.9 1.0 %copy-start = (f32[40,128]{1,0:T(8,128)S(1)}, f32[40,128]{1,0:T(8,128)}, u32[]{:S(2)}) copy-start(f32[40,128]{1,0:T(8,128)} %get-tuple-element.14.tile) | copy-start | bytes 61444
  54.8 11.7 %all-to-all-start.2 = ((f32[4,128,128]{2,1,0:T(8,128)}), f32[4,128,128]{2,1,0:T(8,128)S(1)}, u32[]{:S(2)}, u32[]{:S(2)}) async-start(f32[4,128,128]{2,1,0:T(8,128)} %get-tuple-element.17), calls=%async_computation.2 | async-start | bytes 524288 | tf_op jit(solution)/shard_map/all_to_all | solution.py:218
  66.5 7.2 %collective-permute-start.3 = (f32[4,128,128]{2,1,0:T(8,128)S(1)}, f32[4,128,128]{2,1,0:T(8,128)S(1)}, u32[]{:S(2)}, u32[]{:S(2)}) collective-permute-start(f32[4,128,128]{2,1,0:T(8,128)S(1)} %all-to-all-done.2.mine), channel_id=1, source_target_pairs={{0,1},{1,0},{2,3},{3,2},{4,5},{5,4},{6,7},{7,6},{8,9},{9,8},{10,11... | collective-permute-start | bytes 786440 | tf_op jit(solution)/shard_map/ppermute | solution.py:219

commit v2 on v1

--- a/solution.py
+++ b/solution.py
@@ -32,7 +32,7 @@
     for x in range(NX) for yl in range(NYL)
 ]
 SECOND = [
-    [device(zh, x, yh, yl) for x in turned(NX, FX) for yl in range(NYL)]
+    [device(zh, x, yh, yl) for x in turned(NX, FX) for yl in turned(NYL, 1)]
     for zh in range(NZ) for yh in range(NYH)
 ]
 LINES = [[zl * NC + c for zl in turned(NL, FL)] for c in range(NC)]
@@ -167,7 +167,7 @@
 
 def codes_of(block_row):
     owner, slot = block_row // ROWS, block_row % ROWS
-    piece = (owner // NY - FX) % NX * NYL + owner % NYL
+    piece = (owner // NY - FX) % NX * NYL + (owner - 1) % NYL
     member = (owner // (NX * NY) - FZ) % NZ * NYH + (owner % NY // NYL - FY) % NYH
     return (piece * PIECE + member * BS) * 2**14 + (piece * PIECE + NP * BS + member) * 4 + slot
 

time: 75.3 us -> 76.4 us (1.015)
  starting transfers between devices: 51.2 us -> 52.3 us
where the time goes in v2:
time: 76.4 us; the launch traced here: 75.9 us
  starting transfers between devices  52.3 us (68%)
  waiting for transfers between devices  10.5 us (14%)
  Pallas kernels  8.73 us (11%)
  blocking collectives  2.66 us (3%)
  local copies, waits for them, and re-layouts  1 us (1%)
    all_to_all x1, starting transfers between devices, local(): plane = lax.all_to_all(copies, 'grid', 0, 0, axis_index_groups=FIRST)  20.3 us
    ppermute x3, starting transfers between devices, local(): lax.ppermute(pair, 'depth', [(n, (n + step * NC) % NCG) for n in range(NC...  11.6 us
    pallas_call x6, Pallas kernels, call(): pl.pallas_call(kernel, out_shape=shapes, in_specs=specs, out_specs=[vmem(...  8.73 us
    all_to_all x1, starting transfers between devices, local(): lax.all_to_all(squared, 'depth', 0, 0, axis_index_groups=LINES)  8.32 us
    all_to_all x1, starting transfers between devices, local(): lax.all_to_all(pieces, 'grid', 0, 0, axis_index_groups=SECOND)  6.57 us
    ppermute x1, starting transfers between devices, local(): other = lax.ppermute(mine, 'depth', [(n, n ^ 1) for n in range(NCG)])  5.51 us
    ppermute x3, waiting for transfers between devices, local(): lax.ppermute(pair, 'depth', [(n, (n + step * NC) % NCG) for n in range(NC...  4.61 us
    all_to_all x1, waiting for transfers between devices, local(): plane = lax.all_to_all(copies, 'grid', 0, 0, axis_index_groups=FIRST)  4.16 us
  transfers between devices with their start and end apart: 7, of which 4 were waited for; matrix products, arithmetic and copies ran while one was open for 2% of the time, Pallas kernels for 4%

profile of v2, /device:TPU:1, one launch (start us, length us, event | category | flops | bytes accessed | tf_op | source)
XLA Modules:
  0.0 75.9 jit_solution(12029703914038690290)
XLA Ops:
  0.0 1.7 %pack.1 = (f32[40,128]{1,0:T(8,128)}, f32[12,33,1,128]{3,2,1,0:T(1,128)}) custom-call(s32[1,4]{1,0:T(1,128)} %bitcast.69, s32[4,4]{1,0:T(4,128)} %bitcast.68, f32[4,32,32]{2,1,0:T(8,128)} %bitcast.63), custom_call_target="tpu_custom_call" | custom-call | flops 16777216 | bytes 16464 | tf_op jit(solution)/shard_map/pack/pallas_call | solution.py:155
  1.7 20.3 %all-to-all-start = ((f32[12,33,1,128]{3,2,1,0:T(1,128)}), f32[12,33,1,128]{3,2,1,0:T(1,128)S(1)}, u32[]{:S(2)}, u32[]{:S(2)}) async-start(f32[12,33,1,128]{3,2,1,0:T(1,128)} %get-tuple-element.13), calls=%async_computation | async-start | bytes 405504 | tf_op jit(solution)/shard_map/all_to_all | solution.py:182
  22.0 2.7 %all-gather = f32[80,128]{1,0:T(8,128)S(1)} all-gather(f32[40,128]{1,0:T(8,128)} %get-tuple-element.14.tile), channel_id=2, replica_groups={{0,1},{2,3},{4,5},{6,7},{8,9},{10,11},{12,13},{14,15},{16,17},{18,19},{..., dimensions={0}, use_global_device_ids=true | all-gather | bytes 61440 | tf_op jit(solution)/shard_map/all_gather | solution.py:183
  24.7 4.2 %all-to-all-done.plane = f32[12,33,1,128]{3,2,1,0:T(1,128)S(1)} async-done(((f32[12,33,1,128]{3,2,1,0:T(1,128)}), f32[12,33,1,128]{3,2,1,0:T(1,128)S(1)}, u32[]{:S(2)}, u32[]{:S(2)}) %all-to-all-start) | async-done | bytes 202784 | tf_op jit(solution)/shard_map/all_to_all | solution.py:182
  28.8 1.3 %spread.1 = f32[8,400,128]{2,1,0:T(8,128)} custom-call(f32[12,33,1,128]{3,2,1,0:T(1,128)S(1)} %all-to-all-done.plane), custom_call_target="tpu_custom_call" | custom-call | flops 16777216 | bytes 202752 | tf_op jit(solution)/shard_map/spread/pallas_call | solution.py:155
  30.1 0.0 copy-start.1
  30.1 6.6 %all-to-all-start.1 = ((f32[8,400,128]{2,1,0:T(8,128)}), f32[8,400,128]{2,1,0:T(8,128)S(1)}, u32[]{:S(2)}, u32[]{:S(2)}) async-start(f32[8,400,128]{2,1,0:T(8,128)} %spread.1), calls=%async_computation.1 | async-start | bytes 3276800 | tf_op jit(solution)/shard_map/all_to_all | solution.py:186
  36.7 0.0 copy-done.1
  36.7 7.5 %collective-permute-start.2 = (f32[2,40,128]{2,1,0:T(8,128)S(1)}, f32[2,40,128]{2,1,0:T(8,128)S(1)}, u32[]{:S(2)}, u32[]{:S(2)}) collective-permute-start(f32[2,40,128]{2,1,0:T(8,128)S(1)} %bitcast.56), channel_id=1, source_target_pairs={{0,6},{1,7},{2,0},{3,1},{4,2},{5,3},{6,4},{7,5},{8,14},{9,15},{10,... | collective-permute-start | bytes 122888 | tf_op jit(solution)/shard_map/ppermute | solution.py:189
  44.3 1.9 %collective-permute-start.1 = (f32[2,40,128]{2,1,0:T(8,128)S(1)}, f32[2,40,128]{2,1,0:T(8,128)S(1)}, u32[]{:S(2)}, u32[]{:S(2)}) collective-permute-start(f32[2,40,128]{2,1,0:T(8,128)S(1)} %bitcast.57), channel_id=1, source_target_pairs={{0,4},{1,5},{2,6},{3,7},{4,0},{5,1},{6,2},{7,3},{8,12},{9,13},{10,... | collective-permute-start | bytes 122888 | tf_op jit(solution)/shard_map/ppermute | solution.py:189
  46.2 2.2 %collective-permute-start = (f32[2,40,128]{2,1,0:T(8,128)S(1)}, f32[2,40,128]{2,1,0:T(8,128)S(1)}, u32[]{:S(2)}, u32[]{:S(2)}) collective-permute-start(f32[2,40,128]{2,1,0:T(8,128)S(1)} %bitcast.58), channel_id=1, source_target_pairs={{0,2},{1,3},{2,4},{3,5},{4,6},{5,7},{6,0},{7,1},{8,10},{9,11},{10,... | collective-permute-start | bytes 122888 | tf_op jit(solution)/shard_map/ppermute | solution.py:189
  48.4 0.0 collective-permute-done.2
  48.4 1.8 %collective-permute-done.1 = f32[2,40,128]{2,1,0:T(8,128)S(1)} collective-permute-done((f32[2,40,128]{2,1,0:T(8,128)S(1)}, f32[2,40,128]{2,1,0:T(8,128)S(1)}, u32[]{:S(2)}, u32[]{:S(2)}) %collective-permute-start.1) | collective-permute-done | bytes 40992 | tf_op jit(solution)/shard_map/ppermute | solution.py:189
  50.2 2.8 %collective-permute-done = f32[2,40,128]{2,1,0:T(8,128)S(1)} collective-permute-done((f32[2,40,128]{2,1,0:T(8,128)S(1)}, f32[2,40,128]{2,1,0:T(8,128)S(1)}, u32[]{:S(2)}, u32[]{:S(2)}) %collective-permute-start) | collective-permute-done | bytes 40992 | tf_op jit(solution)/shard_map/ppermute | solution.py:189
  53.0 0.0 copy-start
  53.1 0.1 copy.9
  53.2 0.1 slice.12
  53.3 0.1 copy.10
  53.4 0.1 reshape.133.codes
  53.5 0.3 reshape.134
  53.8 0.2 reshape.135.left
  54.0 0.0 all-to-all-done.1
  54.0 0.0 copy-done
  54.0 1.8 %square.1 = (f32[4,128,128]{2,1,0:T(8,128)}, f32[128,128]{1,0:T(8,128)S(1)}) custom-call(s32[32]{0:T(128)S(1)} %reshape.133.codes, f32[40,128]{1,0:T(8,128)S(1)} %copy-done, f32[4,32,256]{2,1,0:T(8,128)S(1)} %reshape.135.left, f32[3200,128]{1,0:T(8,128)S(1)} %bitcast.50), custom_call_target="tpu_custom_call" | custom-call | flops 16777216 | bytes 1790080 | tf_op jit(solution)/shard_map/square/pallas_call | solution.py:155
  55.9 8.3 %all-to-all-start.2 = ((f32[4,128,128]{2,1,0:T(8,128)}), f32[4,128,128]{2,1,0:T(8,128)S(1)}, u32[]{:S(2)}, u32[]{:S(2)}) async-start(f32[4,128,128]{2,1,0:T(8,128)} %get-tuple-element.17), calls=%async_computation.2 | async-start | bytes 524288 | tf_op jit(solution)/shard_map/all_to_all | solution.py:218
  64.2 0.1 iota_compare_fusion
  64.2 0.2 fusion.14
  64.4 0.1 select_reduce_fusion
  64.6 0.1 reshape.137.codes
  64.7 1.4 %right.2.upper = bf16[2048,256]{1,0:T(8,128)(2,1)S(1)} custom-call(s32[128]{0:T(128)S(1)} %reshape.137.codes, f32[40,128]{1,0:T(8,128)S(1)} %copy-done, f32[3200,128]{1,0:T(8,128)S(1)} %bitcast.51), custom_call_target="tpu_custom_call" | custom-call | flops 16777216 | bytes 1659392 | tf_op jit(solution)/shard_map/right/pallas_call | solution.py:155
  66.1 1.8 %all-to-all-done.2.mine = f32[4,128,128]{2,1,0:T(8,128)S(1)} async-done(((f32[4,128,128]{2,1,0:T(8,128)}), f32[4,128,128]{2,1,0:T(8,128)S(1)}, u32[]{:S(2)}, u32[]{:S(2)}) %all-to-all-start.2) | async-done | bytes 262176 | tf_op jit(solution)/shard_map/all_to_all | solution.py:218
  67.9 5.5 %collective-permute-start.3 = (f32[4,128,128]{2,1,0:T(8,128)S(1)}, f32[4,128,128]{2,1,0:T(8,128)S(1)}, u32[]{:S(2)}, u32[]{:S(2)}) collective-permute-start(f32[4,128,128]{2,1,0:T(8,128)S(1)} %all-to-all-done.2.mine), channel_id=1, source_target_pairs={{0,1},{1,0},{2,3},{3,2},{4,5},{5,4},{6,7},{7,6},{8,9},{9,8},{10,11... | collective-permute-start | bytes 786440 | tf_op jit(solution)/shard_map/ppermute | solution.py:219
  73.4 1.4 %right.3.lower = bf16[2048,256]{1,0:T(8,128)(2,1)S(1)} custom-call(s32[128]{0:T(128)S(1)} %reshape.137.codes, f32[40,128]{1,0:T(8,128)S(1)} %copy-done, f32[3200,128]{1,0:T(8,128)S(1)} %bitcast.52), custom_call_target="tpu_custom_call" | custom-call | flops 16777216 | bytes 1659392 | tf_op jit(solution)/shard_map/right/pallas_call | solution.py:155
  74.8 0.0 collective-permute-done.3.other
  74.8 1.1 %cube.1 = f32[128,128]{1,0:T(8,128)} custom-call(f32[4,128,128]{2,1,0:T(8,128)S(1)} %all-to-all-done.2.mine, f32[4,128,128]{2,1,0:T(8,128)S(1)} %collective-permute-done.3.other, f32[128,128]{1,0:T(8,128)S(1)} %get-tuple-element.19.own, bf16[2048,256]{1,0:T(8,128)(2,1)S(1)} %right.2.upper, bf16[2048,256]{1,0:T(8,128)(2,1)S(1)} %right.3.lower), custom_call_target="tpu_custom_call" | custom-call | flops 16777216 | bytes 4784128 | tf_op jit(solution)/shard_map/cube/pallas_call | solution.py:155
  (11 shorter events, 0.2 us)
Async XLA Ops:
  1.7 27.1 %all-to-all-start = ((f32[12,33,1,128]{3,2,1,0:T(1,128)}), f32[12,33,1,128]{3,2,1,0:T(1,128)S(1)}, u32[]{:S(2)}, u32[]{:S(2)}) async-start(f32[12,33,1,128]{3,2,1,0:T(1,128)} %get-tuple-element.13), calls=%async_computation | async-start | bytes 405504 | tf_op jit(solution)/shard_map/all_to_all | solution.py:182
  30.1 6.6 %copy-start.1 = (s32[4]{0:T(128)S(1)}, s32[4]{0:T(128)}, u32[]{:S(2)}) copy-start(s32[4]{0:T(128)} %constant.252) | copy-start | bytes 52
  30.1 23.8 %all-to-all-start.1 = ((f32[8,400,128]{2,1,0:T(8,128)}), f32[8,400,128]{2,1,0:T(8,128)S(1)}, u32[]{:S(2)}, u32[]{:S(2)}) async-start(f32[8,400,128]{2,1,0:T(8,128)} %spread.1), calls=%async_computation.1 | async-start | bytes 3276800 | tf_op jit(solution)/shard_map/all_to_all | solution.py:186
  36.7 11.7 %collective-permute-start.2 = (f32[2,40,128]{2,1,0:T(8,128)S(1)}, f32[2,40,128]{2,1,0:T(8,128)S(1)}, u32[]{:S(2)}, u32[]{:S(2)}) collective-permute-start(f32[2,40,128]{2,1,0:T(8,128)S(1)} %bitcast.56), channel_id=1, source_target_pairs={{0,6},{1,7},{2,0},{3,1},{4,2},{5,3},{6,4},{7,5},{8,14},{9,15},{10,... | collective-permute-start | bytes 122888 | tf_op jit(solution)/shard_map/ppermute | solution.py:189
  44.3 5.9 %collective-permute-start.1 = (f32[2,40,128]{2,1,0:T(8,128)S(1)}, f32[2,40,128]{2,1,0:T(8,128)S(1)}, u32[]{:S(2)}, u32[]{:S(2)}) collective-permute-start(f32[2,40,128]{2,1,0:T(8,128)S(1)} %bitcast.57), channel_id=1, source_target_pairs={{0,4},{1,5},{2,6},{3,7},{4,0},{5,1},{6,2},{7,3},{8,12},{9,13},{10,... | collective-permute-start | bytes 122888 | tf_op jit(solution)/shard_map/ppermute | solution.py:189
  46.2 6.8 %collective-permute-start = (f32[2,40,128]{2,1,0:T(8,128)S(1)}, f32[2,40,128]{2,1,0:T(8,128)S(1)}, u32[]{:S(2)}, u32[]{:S(2)}) collective-permute-start(f32[2,40,128]{2,1,0:T(8,128)S(1)} %bitcast.58), channel_id=1, source_target_pairs={{0,2},{1,3},{2,4},{3,5},{4,6},{5,7},{6,0},{7,1},{8,10},{9,11},{10,... | collective-permute-start | bytes 122888 | tf_op jit(solution)/shard_map/ppermute | solution.py:189
  53.0 1.0 %copy-start = (f32[40,128]{1,0:T(8,128)S(1)}, f32[40,128]{1,0:T(8,128)}, u32[]{:S(2)}) copy-start(f32[40,128]{1,0:T(8,128)} %get-tuple-element.14.tile) | copy-start | bytes 61444
  55.9 12.0 %all-to-all-start.2 = ((f32[4,128,128]{2,1,0:T(8,128)}), f32[4,128,128]{2,1,0:T(8,128)S(1)}, u32[]{:S(2)}, u32[]{:S(2)}) async-start(f32[4,128,128]{2,1,0:T(8,128)} %get-tuple-element.17), calls=%async_computation.2 | async-start | bytes 524288 | tf_op jit(solution)/shard_map/all_to_all | solution.py:218
  67.9 6.9 %collective-permute-start.3 = (f32[4,128,128]{2,1,0:T(8,128)S(1)}, f32[4,128,128]{2,1,0:T(8,128)S(1)}, u32[]{:S(2)}, u32[]{:S(2)}) collective-permute-start(f32[4,128,128]{2,1,0:T(8,128)S(1)} %all-to-all-done.2.mine), channel_id=1, source_target_pairs={{0,1},{1,0},{2,3},{3,2},{4,5},{5,4},{6,7},{7,6},{8,9},{9,8},{10,11... | collective-permute-start | bytes 786440 | tf_op jit(solution)/shard_map/ppermute | solution.py:219
